TPU v7x, 32 devices: a whole 2x2x4 slice. The times are simulated.
32 devices in a mesh: groups: 2 (over y), context: 4 (over z), tensor: 4 (over x, core).
Axes of the slice: x: 2, y: 2, z: 4, core: 2. Of those that a mesh axis runs over, the one named last changes fastest.
Arguments:
- outer_gate: bfloat16 [1024, 8192], P(('groups', 'context'), 'tensor'), parts along dimension 0, may hold values from -6 to 6
- inner_gate: bfloat16 [1024, 8192], P(('groups', 'context'), 'tensor'), parts along dimension 0, may hold values from -6 to 6
- value_path: bfloat16 [1024, 8192], P(('groups', 'context'), 'tensor'), parts along dimension 0, may hold values from -6 to 6
- long_filter: bfloat16 [512, 8192], P('context', 'tensor'), may hold values from -0.25 to 0.25
- skip_scale: float32 [8192], P('tensor'), may hold values from 0.5 to 1.5
- out_weight: bfloat16 [8192, 8192], P('context'), may hold values from -0.0625 to 0.0625
Outputs:
- projected: bfloat16 [1024, 8192], P(('groups', 'context'), 'tensor'), parts along dimension 0
There are 2 independent parts, one for each index of `groups`. A program takes and returns all parts, laid end to end along the dimension named above; an argument that names none is the same for every part. Nothing has to cross between parts.
All inputs are finite; a program needn't handle non-finite values.
Results may differ from a plain program's by a relative error of at most 0.005.
Values may be sent and summed in bfloat16 or wider, within the bound.
A program may use at most 192 MiB of HBM per device.

v0:
```python
import math

import jax
import jax.numpy as jnp
from jax import lax
from jax.sharding import PartitionSpec as P

precise = lax.Precision.HIGH


def phase_table(row_count, col_count, period, row_start, col_start):
    row_index = lax.iota(jnp.int32, row_count)[:, None] + row_start
    col_index = lax.iota(jnp.int32, col_count)[None, :] + col_start
    angle = (row_index * col_index % period).astype(jnp.float32) * (2.0 * math.pi / period)
    return (jnp.cos(angle), jnp.sin(angle))


def over_blocks(matrix, stacked_rows):
    flattened = stacked_rows.reshape(stacked_rows.shape[0], -1)
    result = jnp.dot(matrix, flattened, precision=precise)
    return result.reshape((matrix.shape[0],) + stacked_rows.shape[1:])


def first_section(signal_rows, period, col_start):
    blocks = signal_rows.shape[0]
    cos_table, sin_table = phase_table(2 * blocks, blocks, 2 * blocks, 0, 0)
    real_part = over_blocks(cos_table, signal_rows)
    imag_part = -over_blocks(sin_table, signal_rows)
    cos_twist, sin_twist = phase_table(2 * blocks, signal_rows.shape[1], period, 0, col_start)
    cos_twist = cos_twist[:, :, None]
    sin_twist = sin_twist[:, :, None]
    return jnp.stack(
        (
            real_part * cos_twist + imag_part * sin_twist,
            imag_part * cos_twist - real_part * sin_twist,
        )
    )


def along_positions(stacked, inverse):
    length = stacked.shape[2]
    cos_table, sin_table = phase_table(length, length, length, 0, 0)
    real_part = stacked[0]
    imag_part = stacked[1]
    cos_real = jnp.einsum("vj,ujc->uvc", cos_table, real_part, precision=precise)
    cos_imag = jnp.einsum("vj,ujc->uvc", cos_table, imag_part, precision=precise)
    sin_real = jnp.einsum("vj,ujc->uvc", sin_table, real_part, precision=precise)
    sin_imag = jnp.einsum("vj,ujc->uvc", sin_table, imag_part, precision=precise)
    if inverse:
        return jnp.stack((cos_real - sin_imag, cos_imag + sin_real))
    return jnp.stack((cos_real + sin_imag, cos_imag - sin_real))


def spectral_product(signal, kernel):
    return jnp.stack(
        (
            signal[0] * kernel[0] - signal[1] * kernel[1],
            signal[0] * kernel[1] + signal[1] * kernel[0],
        )
    )


def inverse_twiddle(stacked, period, row_start):
    cos_twist, sin_twist = phase_table(stacked.shape[1], stacked.shape[2], period, row_start, 0)
    cos_twist = cos_twist[:, :, None]
    sin_twist = sin_twist[:, :, None]
    real_part = stacked[0]
    imag_part = stacked[1]
    return jnp.stack(
        (
            real_part * cos_twist - imag_part * sin_twist,
            real_part * sin_twist + imag_part * cos_twist,
        )
    )


def last_section(stacked, blocks, period):
    cos_table, sin_table = phase_table(blocks, 2 * blocks, 2 * blocks, 0, 0)
    return (over_blocks(cos_table, stacked[0]) - over_blocks(sin_table, stacked[1])) * (
        1.0 / period
    )


def body(outer_gate, inner_gate, value_path, long_filter, skip_scale, out_weight):
    blocks = lax.axis_size("context")
    my_block = lax.axis_index("context")
    positions = inner_gate.shape[0]
    chan_width = inner_gate.shape[1]
    slice_len = positions // blocks
    period = 2 * blocks * positions
    inner_rows, value_rows, filter_rows = (
        lax.all_to_all(inner_gate[None], "context", split_axis=1, concat_axis=0, tiled=True),
        lax.all_to_all(value_path[None], "context", split_axis=1, concat_axis=0, tiled=True),
        lax.all_to_all(long_filter[None], "context", split_axis=1, concat_axis=0, tiled=True),
    )
    mixed_rows = inner_rows.astype(jnp.float32) * value_rows.astype(jnp.float32)
    signal = first_section(mixed_rows, period, my_block * slice_len)
    kernel = first_section(filter_rows.astype(jnp.float32), period, my_block * slice_len)
    signal, kernel = (
        lax.all_to_all(signal, "context", split_axis=1, concat_axis=2, tiled=True),
        lax.all_to_all(kernel, "context", split_axis=1, concat_axis=2, tiled=True),
    )
    spectrum = spectral_product(along_positions(signal, False), along_positions(kernel, False))
    returned = inverse_twiddle(along_positions(spectrum, True), period, 2 * my_block)
    returned = lax.all_to_all(returned, "context", split_axis=2, concat_axis=1, tiled=True)
    conv_rows = last_section(returned, blocks, period)
    conv = lax.all_to_all(conv_rows, "context", split_axis=0, concat_axis=1, tiled=True)[0]
    mixed_local = inner_gate.astype(jnp.float32) * value_path.astype(jnp.float32)
    gated = (outer_gate.astype(jnp.float32) * (conv + skip_scale[None, :] * mixed_local)).astype(
        jnp.bfloat16
    )
    tensor_index = lax.axis_index("tensor")
    features = lax.all_gather(gated, "tensor", axis=1, tiled=True)
    own_columns = lax.dynamic_slice_in_dim(out_weight, tensor_index * chan_width, chan_width, 1)
    return jnp.dot(
        features,
        lax.all_gather(own_columns, "context", axis=0, tiled=True),
        preferred_element_type=jnp.float32,
    ).astype(jnp.bfloat16)


def solution(mesh):
    placed = (
        P(("groups", "context"), "tensor"),
        P(("groups", "context"), "tensor"),
        P(("groups", "context"), "tensor"),
        P("context", "tensor"),
        P("tensor"),
        P("context", None),
    )
    return jax.shard_map(
        body,
        mesh=mesh,
        in_specs=placed,
        out_specs=P(("groups", "context"), "tensor"),
        check_vma=False,
    )
```

profile of v0, /device:TPU:9, one launch (start us, length us, event | category | flops | bytes accessed | tf_op | source)
XLA Modules:
  0.0 1062.8 jit_solution(772707032025125134)
XLA Ops:
  8.9 3.7 reduce.4
  13.8 4.8 all-to-all-start.3
  19.4 3.8 reduce.6
  24.3 4.8 all-to-all-done.3
  29.2 17.9 %all-to-all-start.1 = ((bf16[4,2,32768]{2,1,0:T(2,128)(2,1)}), bf16[4,2,32768]{2,1,0:T(2,128)(2,1)S(1)}, u32[]{:S(2)}, u32[]{:S(2)}) async-start(bf16[4,2,32768]{2,1,0:T(2,128)(2,1)} %reshape.173), calls=%async_computation.1 | async-start | bytes 1048576 | tf_op jit(solution)/shard_map/all_to_all | solution.py:93
  47.9 3.7 reduce.5
  53.5 4.0 all-to-all-done.1
  57.5 7.7 all-to-all-start
  65.2 3.0 bitcast_reduce_fusion
  71.3 2.3 fusion.62
  73.5 2.3 all-to-all-done
  75.8 3.5 reshape.176
  79.3 5.7 multiply_reduce_fusion
  88.5 4.2 add_bitcast_fusion.1
  93.2 4.4 copy.49
  97.6 8.4 all-to-all-start.4
  108.0 4.4 copy.42
  112.4 82.3 %all-to-all-done.4 = f32[2,8,32,2048]{3,2,0,1:T(8,128)} async-done(((f32[2,8,32,2048]{3,2,0,1:T(8,128)}), f32[2,8,32,2048]{3,2,0,1:T(8,128)}, u32[]{:S(2)}, u32[]{:S(2)}) %all-to-all-start.4) | async-done | bytes 4194336 | tf_op jit(solution)/shard_map/all_to_all | solution.py:101
  194.7 8.8 all-to-all-start.2
  204.1 2.5 copy.50
  213.4 3.4 convolution_add_fusion.1
  216.8 75.5 %all-to-all-done.2 = f32[2,8,32,2048]{3,2,0,1:T(8,128)} async-done(((f32[2,8,32,2048]{3,2,0,1:T(8,128)}), f32[2,8,32,2048]{3,2,0,1:T(8,128)}, u32[]{:S(2)}, u32[]{:S(2)}) %all-to-all-start.2) | async-done | bytes 4194336 | tf_op jit(solution)/shard_map/all_to_all | solution.py:100
  292.3 2.5 copy.43
  311.4 7.3 copy.59
  318.7 98.5 %all_to_all.81 = f32[2,2,128,2048]{3,1,0,2:T(2,128)S(1)} all-to-all(f32[2,2,128,2048]{3,1,0,2:T(2,128)} %copy.59), channel_id=1, replica_groups=mesh['groups'=2,'context'=4,'tensor'=4] {'context'}, dimensions={2} | all-to-all | bytes 8388608 | tf_op jit(solution)/shard_map/all_to_all | solution.py:105
  417.2 2.4 copy.60
  422.6 2.3 fusion
  425.6 27.6 %all_to_all.82 = f32[4,32,2048]{2,1,0:T(8,128)S(1)} all-to-all(f32[4,32,2048]{2,1,0:T(8,128)S(1)} %copy.63), channel_id=1, replica_groups=mesh['groups'=2,'context'=4,'tensor'=4] {'context'}, dimensions={0} | all-to-all | bytes 2097152 | tf_op jit(solution)/shard_map/all_to_all | solution.py:107
  454.7 8.3 constant_dynamic-slice_fusion
  463.0 16.5 %all-gather.3.cloned.1.call-done = bf16[128,8192]{1,0:T(8,128)(2,1)} async-done(((bf16[128,2048]{1,0:T(8,128)(2,1)}), bf16[128,8192]{1,0:T(8,128)(2,1)}) %all-gather.3.cloned.1.call-update) | async-done | bytes 2097168 | tf_op jit(solution)/shard_map/all_gather | solution.py:113
  479.5 559.8 %all-gather.5.cloned.1.call-done = bf16[8192,2048]{1,0:T(8,128)(2,1)} async-done(((bf16[2048,2048]{1,0:T(8,128)(2,1)}), bf16[8192,2048]{1,0:T(8,128)(2,1)}) %all-gather.5.cloned.1.call-update) | async-done | bytes 33554448 | tf_op jit(solution)/shard_map/all_gather | solution.py:117
  1039.2 16.5 %convolution_convert_fusion = bf16[128,2048]{1,0:T(8,128)(2,1)} fusion(bf16[128,8192]{1,0:T(8,128)(2,1)} %all-gather.3.cloned.1.call-done, bf16[8192,2048]{1,0:T(8,128)(2,1)} %all-gather.5.cloned.1.call-done), kind=kOutput, calls=%fused_computation.13 | convolution fusion | flops 4295229440 | bytes 36175872 | tf_op jit(solution)/shard_map/dot_general | solution.py:115
  (67 shorter events, 46.2 us)
Async XLA Ops:
  8.4 10.2 copy-start.6
  13.8 15.4 %all-to-all-start.3 = ((bf16[4,2,32768]{2,1,0:T(2,128)(2,1)}), bf16[4,2,32768]{2,1,0:T(2,128)(2,1)S(1)}, u32[]{:S(2)}, u32[]{:S(2)}) async-start(bf16[4,2,32768]{2,1,0:T(2,128)(2,1)} %reshape.177), calls=%async_computation.3 | async-start | bytes 1048576 | tf_op jit(solution)/shard_map/all_to_all | solution.py:94
  19.4 27.7 %copy-start.4 = (bf16[128,2048]{1,0:T(8,128)(2,1)S(1)}, bf16[128,2048]{1,0:T(8,128)(2,1)}, u32[]{:S(2)}) copy-start(bf16[128,2048]{1,0:T(8,128)(2,1)} %param.7) | copy-start | bytes 1572868
  29.2 28.3 %all-to-all-start.1 = ((bf16[4,2,32768]{2,1,0:T(2,128)(2,1)}), bf16[4,2,32768]{2,1,0:T(2,128)(2,1)S(1)}, u32[]{:S(2)}, u32[]{:S(2)}) async-start(bf16[4,2,32768]{2,1,0:T(2,128)(2,1)} %reshape.173), calls=%async_computation.1 | async-start | bytes 1048576 | tf_op jit(solution)/shard_map/all_to_all | solution.py:93
  57.5 18.3 %all-to-all-start = ((bf16[4,2,32768]{2,1,0:T(2,128)(2,1)}), bf16[4,2,32768]{2,1,0:T(2,128)(2,1)}, u32[]{:S(2)}, u32[]{:S(2)}) async-start(bf16[4,2,32768]{2,1,0:T(2,128)(2,1)} %reshape.175), calls=%async_computation | async-start | bytes 1048576 | tf_op jit(solution)/shard_map/all_to_all | solution.py:92
  73.5 5.7 copy-start.3
  86.9 1.6 copy-start.1
  97.6 8.4 copy-start.2
  97.6 97.1 %all-to-all-start.4 = ((f32[2,8,32,2048]{3,2,0,1:T(8,128)}), f32[2,8,32,2048]{3,2,0,1:T(8,128)}, u32[]{:S(2)}, u32[]{:S(2)}) async-start(f32[2,8,32,2048]{3,2,0,1:T(8,128)} %copy.49), calls=%async_computation.4 | async-start | bytes 8388608 | tf_op jit(solution)/shard_map/all_to_all | solution.py:101
  194.7 97.5 %all-to-all-start.2 = ((f32[2,8,32,2048]{3,2,0,1:T(8,128)}), f32[2,8,32,2048]{3,2,0,1:T(8,128)}, u32[]{:S(2)}, u32[]{:S(2)}) async-start(f32[2,8,32,2048]{3,2,0,1:T(8,128)} %copy.42), calls=%async_computation.2 | async-start | bytes 8388608 | tf_op jit(solution)/shard_map/all_to_all | solution.py:100
  203.6 275.9 %all-gather.3.cloned.1.call-start = ((), (), s32[]{:S(2)}) async-start(), calls=%async_computation.7 | async-start | bytes 2621440 | tf_op jit(solution)/shard_map/all_gather | solution.py:113
  299.8 2.0 copy-start
  424.9 28.3 %copy-start.5 = (bf16[128,2048]{1,0:T(8,128)(2,1)S(1)}, bf16[128,2048]{1,0:T(8,128)(2,1)}, u32[]{:S(2)}) copy-start(bf16[128,2048]{1,0:T(8,128)(2,1)} %param.7) | copy-start | bytes 1572868
  424.9 28.3 %copy-start.7 = (bf16[128,2048]{1,0:T(8,128)(2,1)S(1)}, bf16[128,2048]{1,0:T(8,128)(2,1)}, u32[]{:S(2)}) copy-start(bf16[128,2048]{1,0:T(8,128)(2,1)} %param.8) | copy-start | bytes 1572868
  424.9 28.3 %copy-start.8 = (bf16[128,2048]{1,0:T(8,128)(2,1)S(1)}, bf16[128,2048]{1,0:T(8,128)(2,1)}, u32[]{:S(2)}) copy-start(bf16[128,2048]{1,0:T(8,128)(2,1)} %param.6) | copy-start | bytes 1572868
  424.9 28.3 %copy-start.9 = (f32[2048]{0:T(1024)S(1)}, f32[2048]{0:T(1024)}, u32[]{:S(2)}) copy-start(f32[2048]{0:T(1024)} %param.10) | copy-start | bytes 24580
  454.4 584.9 %all-gather.5.cloned.1.call-start = ((), (), s32[]{:S(2)}) async-start(), calls=%async_computation.8 | async-start | bytes 41943040 | tf_op jit(solution)/shard_map/all_gather | solution.py:117
Sparse Core Ops, SparseCore 0:
  454.5 24.9 all-gather.2
  481.0 558.1 all-gather.4
where the time goes:
time: 1070 us; the launch traced here: 1060 us
  waiting for transfers between devices  745 us (70%)
  blocking collectives  126 us (12%)
  local copies, waits for them, and re-layouts  54.2 us (5%)
  matrix products  52 us (5%)
  starting transfers between devices  48.3 us (5%)
  other arithmetic  22.9 us (2%)
  between operations  14.1 us (1%)
    all_gather x1, waiting for transfers between devices, body(): lax.all_gather(own_columns, 'context', axis=0, tiled=True)  560 us
    all_to_all x1, blocking collectives, body(): lax.all_to_all(returned, 'context', split_axis=2, concat_axis=1, tiled=True)  98.5 us
    all_to_all x1, waiting for transfers between devices, body(): lax.all_to_all(kernel, 'context', split_axis=1, concat_axis=2, tiled=True)  82.3 us
    all_to_all x1, waiting for transfers between devices, body(): lax.all_to_all(signal, 'context', split_axis=1, concat_axis=2, tiled=True)  75.5 us
    all_to_all x1, blocking collectives, body(): lax.all_to_all(conv_rows, 'context', split_axis=0, concat_axis=1, tiled=T...  27.6 us
  transfers between devices with their start and end apart: 7, of which 7 were waited for; matrix products, arithmetic and copies ran while one was open for 4% of the time, Pallas kernels for 0%

commit v1 on v0

v1 whole, which is shorter than its diff:
```python
import math

import jax
import jax.numpy as jnp
import ml_dtypes
import numpy as np
from jax import lax
from jax.sharding import PartitionSpec as P


def transform_tables(length):
    index = np.arange(length, dtype=np.int64)
    turns = ((4 * index[:, None] + 1) * index[None, :]) % (4 * length)
    angle = turns * (2.0 * math.pi / (4 * length))
    table = np.concatenate([np.cos(angle), -np.sin(angle)], axis=0)
    high = table.astype(ml_dtypes.bfloat16)
    low = (table - high.astype(np.float64)).astype(ml_dtypes.bfloat16)
    return high, low


def mm(a, b):
    return jnp.dot(a, b, preferred_element_type=jnp.float32)


def causal_conv(high, low, high_t, low_t, signal, kernel):
    length = signal.shape[0]
    spec_s = mm(high, signal) + mm(low, signal)
    spec_k = mm(high, kernel) + mm(low, kernel)
    s_re, s_im = spec_s[:length], spec_s[length:]
    k_re, k_im = spec_k[:length], spec_k[length:]
    prod = jnp.concatenate([s_re * k_re - s_im * k_im, s_re * k_im + s_im * k_re], axis=0)
    p_high = prod.astype(jnp.bfloat16)
    p_low = (prod - p_high.astype(jnp.float32)).astype(jnp.bfloat16)
    return (mm(high_t, p_high) + mm(low_t, p_high) + mm(high_t, p_low)) * (1.0 / length)


def body(outer_gate, inner_gate, value_path, long_filter, skip_scale, out_weight):
    n_ctx = lax.axis_size("context")
    n_ten = lax.axis_size("tensor")
    ctx = lax.axis_index("context")
    ten = lax.axis_index("tensor")
    positions, width = inner_gate.shape
    sub = width // n_ctx
    length = n_ctx * positions
    high, low = transform_tables(length)
    mixed = (inner_gate.astype(jnp.float32) * value_path.astype(jnp.float32)).astype(jnp.bfloat16)
    stacked = jnp.stack([mixed, outer_gate, long_filter])
    stacked = lax.all_to_all(stacked, "context", split_axis=2, concat_axis=1, tiled=True)
    signal, outer, kernel = stacked[0], stacked[1], stacked[2]
    conv = causal_conv(high, low, np.ascontiguousarray(high.T), np.ascontiguousarray(low.T), signal, kernel)
    skip = lax.dynamic_slice_in_dim(skip_scale, ctx * sub, sub, 0)
    gated = (
        outer.astype(jnp.float32) * (conv + skip[None, :] * signal.astype(jnp.float32))
    ).astype(jnp.bfloat16)
    pairs = [(c * n_ten + t, t * n_ctx + c) for c in range(n_ctx) for t in range(n_ten)]
    gated = lax.ppermute(gated, ("context", "tensor"), pairs)
    features = lax.all_gather(gated, "tensor", axis=1, tiled=True)
    columns = out_weight.shape[1] // n_ten
    own = lax.dynamic_slice_in_dim(out_weight, ten * columns, columns, 1)
    partial = mm(features, own).astype(jnp.bfloat16).reshape(n_ctx, positions, columns)
    partial = lax.all_to_all(partial, "context", split_axis=0, concat_axis=0, tiled=True)
    return jnp.sum(partial.astype(jnp.float32), axis=0).astype(jnp.bfloat16)


def solution(mesh):
    placed = (
        P(("groups", "context"), "tensor"),
        P(("groups", "context"), "tensor"),
        P(("groups", "context"), "tensor"),
        P("context", "tensor"),
        P("tensor"),
        P("context", None),
    )
    return jax.shard_map(
        body,
        mesh=mesh,
        in_specs=placed,
        out_specs=P(("groups", "context"), "tensor"),
        check_vma=False,
    )
```

time: 1070 us -> 197 us (0.18)
  the two profiles are of different devices: /device:TPU:9 before, /device:TPU:0 now
where the time goes in v1:
time: 197 us; the launch traced here: 196 us
  waiting for transfers between devices  93.5 us (47%)
  blocking collectives  53 us (27%)
  matrix products  14 us (7%)
  between operations  13.6 us (7%)
  local copies, waits for them, and re-layouts  9.41 us (5%)
  starting transfers between devices  7.19 us (4%)
  other arithmetic  5.44 us (3%)
    all_to_all x1, blocking collectives, body(): lax.all_to_all(partial, 'context', split_axis=0, concat_axis=0, tiled=True)  53 us
    all_to_all x1, waiting for transfers between devices, body(): lax.all_to_all(stacked, 'context', split_axis=2, concat_axis=1, tiled=True)  47.4 us
    all_gather x1, waiting for transfers between devices, body(): features = lax.all_gather(gated, 'tensor', axis=1, tiled=True)  46.1 us
    dot_general x8, matrix products, mm(): return jnp.dot(a, b, preferred_element_type=jnp.float32)  14 us
    all_to_all x1, starting transfers between devices, body(): lax.all_to_all(stacked, 'context', split_axis=2, concat_axis=1, tiled=True)  6.32 us
  transfers between devices with their start and end apart: 3, of which 2 were waited for; matrix products, arithmetic and copies ran while one was open for 0% of the time, Pallas kernels for 0%

profile of v1, /device:TPU:0, one launch (start us, length us, event | category | flops | bytes accessed | tf_op | source)
XLA Modules:
  0.0 196.1 jit_solution(17265750976352935905)
XLA Ops:
  6.5 1.3 fusion.11
  7.9 1.4 pad_maximum_fusion.1
  9.2 2.5 %copy.30 = bf16[3,128,2048]{1,0,2:T(4,128)(2,1)} copy(bf16[3,128,2048]{2,1,0:T(8,128)(2,1)S(1)} %pad_maximum_fusion.1) | data formatting | bytes 3145728 | tf_op jit(solution)/shard_map/stack | solution.py:47
  11.8 6.3 %all-to-all-start = ((bf16[3,128,2048]{1,0,2:T(4,128)(2,1)}), bf16[3,128,2048]{1,0,2:T(4,128)(2,1)S(1)}, u32[]{:S(2)}, u32[]{:S(2)}) async-start(bf16[3,128,2048]{1,0,2:T(4,128)(2,1)} %copy.30), calls=%async_computation | async-start | bytes 4194304 | tf_op jit(solution)/shard_map/all_to_all | solution.py:48
  18.1 0.8 dynamic_slice.6
  18.8 47.4 %all-to-all-done = bf16[3,128,2048]{1,0,2:T(4,128)(2,1)S(1)} async-done(((bf16[3,128,2048]{1,0,2:T(4,128)(2,1)}), bf16[3,128,2048]{1,0,2:T(4,128)(2,1)S(1)}, u32[]{:S(2)}, u32[]{:S(2)}) %all-to-all-start) | async-done | bytes 1572896 | tf_op jit(solution)/shard_map/all_to_all | solution.py:48
  66.3 0.2 copy.31
  66.5 0.9 fusion.20
  67.4 0.3 copy.32
  67.8 0.3 copy.36
  68.1 0.2 copy.34
  68.3 1.3 copy.33
  69.7 1.0 copy.35
  70.7 0.8 fusion.21
  71.5 0.8 fusion.22
  72.2 0.5 copy-done.2
  72.7 0.8 add_bitcast_fusion
  73.4 0.8 add_bitcast_fusion.1
  74.2 0.5 multiply_subtract_fusion
  74.7 0.7 copy-done.1
  75.4 0.7 fusion.14
  76.2 0.5 copy-done.4
  76.7 0.8 convolution_add_fusion.1
  77.4 0.3 copy-done.3
  77.7 0.9 fusion.10
  78.6 0.9 collective-permute-start
  79.5 0.8 copy-done.5
  80.3 0.0 all-gather.2.cloned.1.call-update
  80.3 46.1 %all-gather.2.cloned.1.call-done = bf16[512,2048]{0,1:T(8,128)(2,1)} async-done(((bf16[512,512]{0,1:T(8,128)(2,1)}), bf16[512,2048]{0,1:T(8,128)(2,1)}) %all-gather.2.cloned.1.call-update) | async-done | bytes 2097168 | tf_op jit(solution)/shard_map/all_gather | solution.py:57
  126.4 8.6 %fusion.2 = bf16[512,2048]{1,0:T(8,128)(2,1)S(1)} fusion(bf16[512,2048]{0,1:T(8,128)(2,1)} %all-gather.2.cloned.1.call-done, bf16[2048,8192]{1,0:T(8,128)(2,1)} %param.15, s32[]{:T(128)S(6)} %select_n.7), kind=kOutput, calls=%fused_computation.2 | convolution fusion | flops 4296015872 | bytes 12582916 | tf_op jit(solution)/shard_map/dot_general | solution.py:22
  134.9 53.0 %all_to_all.20 = bf16[4,128,2048]{2,1,0:T(8,128)(2,1)S(1)} all-to-all(bf16[4,128,2048]{2,1,0:T(8,128)(2,1)S(1)} %bitcast.42), channel_id=1, replica_groups=mesh['groups'=2,'context'=4,'tensor'=4] {'context'}, dimensions={0} | all-to-all | bytes 4194304 | tf_op jit(solution)/shard_map/all_to_all | solution.py:61
  187.9 1.3 reduce_sum.12
  (9 shorter events, 0.0 us)
Async XLA Ops:
  11.8 54.5 %all-to-all-start = ((bf16[3,128,2048]{1,0,2:T(4,128)(2,1)}), bf16[3,128,2048]{1,0,2:T(4,128)(2,1)S(1)}, u32[]{:S(2)}, u32[]{:S(2)}) async-start(bf16[3,128,2048]{1,0,2:T(4,128)(2,1)} %copy.30), calls=%async_computation | async-start | bytes 4194304 | tf_op jit(solution)/shard_map/all_to_all | solution.py:48
  18.1 108.3 %all-gather.2.cloned.1.call-start = ((), (), s32[]{:S(2)}) async-start(), calls=%async_computation.2 | async-start | bytes 2621440 | tf_op jit(solution)/shard_map/all_gather | solution.py:57
  68.1 2.6 %copy-start = (bf16[1024,512]{1,0:T(8,128)(2,1)S(1)}, bf16[1024,512]{1,0:T(8,128)(2,1)}, u32[]{:S(2)}) copy-start(bf16[1024,512]{1,0:T(8,128)(2,1)} %constant.28.clone) | copy-start | bytes 3145732
  71.4 1.2 copy-start.2
  74.2 1.2 copy-start.1
  75.4 1.2 copy-start.4
  76.7 1.0 copy-start.3
  78.6 0.9 collective-permute-start
  79.5 0.8 copy-start.5
Sparse Core Ops, SparseCore 0:
  80.4 45.9 all-gather.1

commit v2 on v1

--- a/solution.py
+++ b/solution.py
@@ -1,3 +1,4 @@
+import functools
 import math
 
 import jax
@@ -5,6 +6,8 @@
 import ml_dtypes
 import numpy as np
 from jax import lax
+from jax.experimental import pallas as pl
+from jax.experimental.pallas import tpu as pltpu
 from jax.sharding import PartitionSpec as P
 
 
@@ -34,7 +37,7 @@
     return (mm(high_t, p_high) + mm(low_t, p_high) + mm(high_t, p_low)) * (1.0 / length)
 
 
-def body(outer_gate, inner_gate, value_path, long_filter, skip_scale, out_weight):
+def body_plain(outer_gate, inner_gate, value_path, long_filter, skip_scale, out_weight):
     n_ctx = lax.axis_size("context")
     n_ten = lax.axis_size("tensor")
     ctx = lax.axis_index("context")
@@ -62,6 +65,239 @@
     return jnp.sum(partial.astype(jnp.float32), axis=0).astype(jnp.bfloat16)
 
 
+MESH = pl.DeviceIdType.MESH
+PARTS = 2
+BLOCK = 128
+TILE = 256
+
+
+def blocked_tables(length):
+    high, low = transform_tables(length)
+
+    def order(table):
+        halves = table.reshape(2, length // BLOCK, BLOCK, length)
+        return np.ascontiguousarray(halves.transpose(1, 0, 2, 3).reshape(2 * length, length))
+
+    high, low = order(high), order(low)
+    return high, low, np.ascontiguousarray(high.T), np.ascontiguousarray(low.T)
+
+
+def fused(
+    n_ctx, n_ten,
+    outer_ref, inner_ref, value_ref, filter_ref, skip_ref, w_hbm, fh_hbm, fl_hbm, gh_hbm, gl_hbm,
+    out_ref,
+    w, fh, fl, gh, gl, stage, rx, skip_stage, skip_rx, acc, feats, pbuf, rbuf, own,
+    load_sem, send1, recv1, send_skip, recv_skip, send2, recv2, send3, recv3,
+):
+    ctx = lax.axis_index("context")
+    ten = lax.axis_index("tensor")
+    grp = lax.axis_index("groups")
+    me = ctx * n_ten + ten
+    total = n_ctx * n_ten
+    positions, width = inner_ref.shape
+    sub = width // n_ctx
+    part = sub // PARTS
+    length = n_ctx * positions
+    columns = w.shape[1]
+
+    loads = [
+        pltpu.make_async_copy(a, b, load_sem.at[i])
+        for i, (a, b) in enumerate(
+            [
+                (fh_hbm, fh), (fl_hbm, fl), (gh_hbm, gh), (gl_hbm, gl),
+                (w_hbm.at[:, pl.ds(pl.multiple_of(ten * columns, 128), columns)], w),
+            ]
+        )
+    ]
+    for load in loads:
+        load.start()
+
+    barrier = pltpu.get_barrier_semaphore()
+    for d in range(1, total):
+        other = lax.rem(me + d, total)
+        pl.semaphore_signal(
+            barrier, inc=1, device_id=(grp, other // n_ten, lax.rem(other, n_ten)), device_id_type=MESH
+        )
+    stage[0] = (inner_ref[...].astype(jnp.float32) * value_ref[...].astype(jnp.float32)).astype(jnp.bfloat16)
+    stage[1] = outer_ref[...]
+    stage[2] = filter_ref[...]
+    skip_stage[...] = jnp.broadcast_to(skip_ref[...], skip_stage.shape)
+    pl.semaphore_wait(barrier, total - 1)
+
+    def input_copies(j):
+        unit = ten * n_ctx + j
+        to = (grp, unit // n_ten, lax.rem(unit, n_ten))
+        pieces = []
+        for h in range(PARTS):
+            pieces.append((
+                stage.at[:, :, pl.ds(j * sub + h * part, part)],
+                rx.at[h, :, pl.ds(pl.multiple_of(ctx * positions, positions), positions), :],
+                send1.at[h, j], recv1.at[h, ctx],
+            ))
+        pieces.append((
+            skip_stage.at[:, pl.ds(j * sub, sub)], skip_rx.at[ctx], send_skip.at[j], recv_skip.at[ctx],
+        ))
+        return unit, to, pieces
+
+    def remote(piece, to):
+        a, b, s, r = piece
+        return pltpu.make_async_remote_copy(
+            src_ref=a, dst_ref=b, send_sem=s, recv_sem=r, device_id=to, device_id_type=MESH
+        )
+
+    for i in [PARTS] + list(range(PARTS)):
+        for j in range(n_ctx):
+            unit, to, pieces = input_copies(j)
+
+            @pl.when(unit != me)
+            def _():
+                remote(pieces[i], to).start()
+
+            @pl.when(unit == me)
+            def _():
+                a, b, s, r = pieces[i]
+                pltpu.make_async_copy(a, b, r).start()
+
+    for load in loads[:4]:
+        load.wait()
+
+    def landed(ref, sem):
+        pltpu.make_async_copy(ref, ref, sem).wait()
+
+    for p in range(n_ctx):
+        landed(skip_rx.at[p], recv_skip.at[p])
+
+    def gather_copy(h, k):
+        here = feats.at[:, pl.ds(pl.multiple_of(ten * sub + h * part, 128), part)]
+        return pltpu.make_async_remote_copy(
+            src_ref=here, dst_ref=here, send_sem=send2.at[h, k], recv_sem=recv2.at[h, k],
+            device_id=(grp, ctx, lax.rem(ten + k, n_ten)), device_id_type=MESH,
+        )
+
+    for h in range(PARTS):
+        for p in range(n_ctx):
+            landed(rx.at[h, :, pl.ds(p * positions, positions), :], recv1.at[h, p])
+        acc[...] = jnp.zeros_like(acc)
+
+        @pl.loop(0, length // BLOCK)
+        def _(b):
+            rows = pl.ds(pl.multiple_of(b * 2 * BLOCK, 2 * BLOCK), 2 * BLOCK)
+            f_high, f_low = fh[rows, :], fl[rows, :]
+            signal, kernel = rx[h, 0], rx[h, 2]
+            spec_s = mm(f_high, signal) + mm(f_low, signal)
+            spec_k = mm(f_high, kernel) + mm(f_low, kernel)
+            s_re, s_im = spec_s[:BLOCK], spec_s[BLOCK:]
+            k_re, k_im = spec_k[:BLOCK], spec_k[BLOCK:]
+            prod = jnp.concatenate([s_re * k_re - s_im * k_im, s_re * k_im + s_im * k_re], axis=0)
+            p_high = prod.astype(jnp.bfloat16)
+            p_low = (prod - p_high.astype(jnp.float32)).astype(jnp.bfloat16)
+            g_high, g_low = gh[:, rows], gl[:, rows]
+            acc[...] += mm(g_high, p_high) + mm(g_low, p_high) + mm(g_high, p_low)
+
+        skip = skip_rx[0, 0:1, h * part:(h + 1) * part]
+        gated = rx[h, 1].astype(jnp.float32) * (
+            acc[...] * (1.0 / length) + skip * rx[h, 0].astype(jnp.float32)
+        )
+        feats[:, pl.ds(pl.multiple_of(ten * sub + h * part, 128), part)] = gated.astype(jnp.bfloat16)
+        for k in range(1, n_ten):
+            gather_copy(h, k).start()
+
+    loads[4].wait()
+    for h in range(PARTS):
+        for k in range(1, n_ten):
+            came = lax.rem(ten + n_ten - k, n_ten)
+            landed(feats.at[:, pl.ds(pl.multiple_of(came * sub + h * part, 128), part)], recv2.at[h, k])
+
+    def partial_copy(k):
+        return pltpu.make_async_remote_copy(
+            src_ref=pbuf.at[k], dst_ref=rbuf.at[k], send_sem=send3.at[k], recv_sem=recv3.at[k],
+            device_id=(grp, lax.rem(ctx + k, n_ctx), ten), device_id_type=MESH,
+        )
+
+    order = sorted(range(1, n_ctx), key=lambda k: abs(k - n_ctx / 2))
+    for k in order + [0]:
+        q = lax.rem(ctx + k, n_ctx)
+        rows = pl.ds(pl.multiple_of(q * positions, positions), positions)
+
+        @pl.loop(0, columns // TILE)
+        def _(n):
+            cols = pl.ds(pl.multiple_of(n * TILE, TILE), TILE)
+            product = mm(feats[rows, :], w[:, cols])
+            if k == 0:
+                own[:, cols] = product
+            else:
+                pbuf[k, :, cols] = product.astype(jnp.bfloat16)
+
+        if k:
+            partial_copy(k).start()
+
+    result = own[...]
+    for k in order:
+        landed(rbuf.at[k], recv3.at[k])
+        result = result + rbuf[k].astype(jnp.float32)
+    out_ref[...] = result.astype(jnp.bfloat16)
+
+    for i in range(PARTS + 1):
+        for j in range(n_ctx):
+            unit, to, pieces = input_copies(j)
+
+            @pl.when(unit != me)
+            def _():
+                remote(pieces[i], to).wait_send()
+    for h in range(PARTS):
+        for k in range(1, n_ten):
+            gather_copy(h, k).wait_send()
+    for k in order:
+        partial_copy(k).wait_send()
+
+
+def body(outer_gate, inner_gate, value_path, long_filter, skip_scale, out_weight):
+    n_ctx = lax.axis_size("context")
+    n_ten = lax.axis_size("tensor")
+    positions, width = inner_gate.shape
+    sub = width // n_ctx
+    length = n_ctx * positions
+    columns = out_weight.shape[1] // n_ten
+    if sub % (PARTS * 128) or length % BLOCK or columns % TILE or positions % 16 or length > 1024:
+        return body_plain(outer_gate, inner_gate, value_path, long_filter, skip_scale, out_weight)
+    tables = [jnp.asarray(t) for t in blocked_tables(length)]
+    bf16, f32 = jnp.bfloat16, jnp.float32
+    part = sub // PARTS
+    dma = pltpu.SemaphoreType.DMA
+    vmem = pl.BlockSpec(memory_space=pltpu.VMEM)
+    hbm = pl.BlockSpec(memory_space=pl.ANY)
+    return pl.pallas_call(
+        functools.partial(fused, n_ctx, n_ten),
+        out_shape=jax.ShapeDtypeStruct((positions, columns), bf16),
+        in_specs=[vmem] * 5 + [hbm] * 5,
+        out_specs=vmem,
+        scratch_shapes=[
+            pltpu.VMEM((out_weight.shape[0], columns), bf16),
+            pltpu.VMEM((2 * length, length), bf16),
+            pltpu.VMEM((2 * length, length), bf16),
+            pltpu.VMEM((length, 2 * length), bf16),
+            pltpu.VMEM((length, 2 * length), bf16),
+            pltpu.VMEM((3, positions, width), bf16),
+            pltpu.VMEM((PARTS, 3, length, part), bf16),
+            pltpu.VMEM((8, width), f32),
+            pltpu.VMEM((n_ctx, 8, sub), f32),
+            pltpu.VMEM((length, part), f32),
+            pltpu.VMEM((length, n_ten * sub), bf16),
+            pltpu.VMEM((n_ctx, positions, columns), bf16),
+            pltpu.VMEM((n_ctx, positions, columns), bf16),
+            pltpu.VMEM((positions, columns), f32),
+            dma((5,)),
+            dma((PARTS, n_ctx)), dma((PARTS, n_ctx)),
+            dma((n_ctx,)), dma((n_ctx,)),
+            dma((PARTS, n_ten)), dma((PARTS, n_ten)),
+            dma((n_ctx,)), dma((n_ctx,)),
+        ],
+        compiler_params=pltpu.CompilerParams(
+            collective_id=0, has_side_effects=True, vmem_limit_bytes=56 * 1024 * 1024
+        ),
+    )(outer_gate, inner_gate, value_path, long_filter, skip_scale[None, :], out_weight, *tables)
+
+
 def solution(mesh):
     placed = (
         P(("groups", "context"), "tensor"),

time: 197 us -> 142 us (0.72)
  the two profiles are of different devices: /device:TPU:0 before, /device:TPU:9 now
where the time goes in v2:
time: 142 us
  Pallas kernels  140 us (99%)
  local copies, waits for them, and re-layouts  1.88 us (1%)
    pallas_call x1, Pallas kernels, body(): pl.pallas_call(functools.partial(fused, n_ctx, n_ten), out_shape=jax.Shap...  140 us

profile of v2, /device:TPU:9, one launch (start us, length us, event | category | flops | bytes accessed | tf_op | source)
XLA Modules:
  0.0 141.5 jit_solution(5176748094225811085)
XLA Ops:
  0.0 139.7 %shard_map.100 = bf16[128,2048]{1,0:T(8,128)(2,1)} custom-call(bf16[128,2048]{1,0:T(8,128)(2,1)} %outer_ref.1, bf16[128,2048]{1,0:T(8,128)(2,1)} %inner_ref.1, bf16[128,2048]{1,0:T(8,128)(2,1)} %value_ref.1, bf16[128,2048]{1,0:T(8,128)(2,1)} %filter_ref.1, f32[1,2048]{1,0:T(1,128)} %bitcast.1, bf16[2048,8192]{1,0:T(8,128)(2,1)} %w_hbm.1, ...), custom_call_target="tpu_custom_call" | custom-call | tf_op jit(solution)/shard_map/pallas_call | solution.py:269
  139.7 1.9 %copy.12 = bf16[128,2048]{1,0:T(8,128)(2,1)} copy(bf16[128,2048]{1,0:T(8,128)(2,1)} %shard_map.100) | data formatting | bytes 1048576

commit v3 on v2

--- a/solution.py
+++ b/solution.py
@@ -86,14 +86,12 @@
     n_ctx, n_ten,
     outer_ref, inner_ref, value_ref, filter_ref, skip_ref, w_hbm, fh_hbm, fl_hbm, gh_hbm, gl_hbm,
     out_ref,
-    w, fh, fl, gh, gl, stage, rx, skip_stage, skip_rx, acc, feats, pbuf, rbuf, own,
-    load_sem, send1, recv1, send_skip, recv_skip, send2, recv2, send3, recv3,
+    w, fh, fl, gh, gl, stage, mid, rx, skip_stage, skip_rx, acc, feats, pbuf, rbuf, own,
+    load_sem, send_x, recv_x, send1, recv1, send_skip, recv_skip, send2, recv2, send3, recv3,
 ):
     ctx = lax.axis_index("context")
     ten = lax.axis_index("tensor")
     grp = lax.axis_index("groups")
-    me = ctx * n_ten + ten
-    total = n_ctx * n_ten
     positions, width = inner_ref.shape
     sub = width // n_ctx
     part = sub // PARTS
@@ -113,59 +111,89 @@
         load.start()
 
     barrier = pltpu.get_barrier_semaphore()
-    for d in range(1, total):
-        other = lax.rem(me + d, total)
+    for k in range(1, n_ten):
         pl.semaphore_signal(
-            barrier, inc=1, device_id=(grp, other // n_ten, lax.rem(other, n_ten)), device_id_type=MESH
+            barrier, inc=1, device_id=(grp, ctx, lax.rem(ten + k, n_ten)), device_id_type=MESH
+        )
+    for k in range(1, n_ctx):
+        pl.semaphore_signal(
+            barrier, inc=1, device_id=(grp, lax.rem(ctx + k, n_ctx), ten), device_id_type=MESH
         )
     stage[0] = (inner_ref[...].astype(jnp.float32) * value_ref[...].astype(jnp.float32)).astype(jnp.bfloat16)
     stage[1] = outer_ref[...]
     stage[2] = filter_ref[...]
     skip_stage[...] = jnp.broadcast_to(skip_ref[...], skip_stage.shape)
-    pl.semaphore_wait(barrier, total - 1)
-
-    def input_copies(j):
-        unit = ten * n_ctx + j
-        to = (grp, unit // n_ten, lax.rem(unit, n_ten))
-        pieces = []
-        for h in range(PARTS):
-            pieces.append((
-                stage.at[:, :, pl.ds(j * sub + h * part, part)],
-                rx.at[h, :, pl.ds(pl.multiple_of(ctx * positions, positions), positions), :],
-                send1.at[h, j], recv1.at[h, ctx],
-            ))
-        pieces.append((
-            skip_stage.at[:, pl.ds(j * sub, sub)], skip_rx.at[ctx], send_skip.at[j], recv_skip.at[ctx],
-        ))
-        return unit, to, pieces
+    pl.semaphore_wait(barrier, n_ten + n_ctx - 2)
+
+    def landed(ref, sem):
+        pltpu.make_async_copy(ref, ref, sem).wait()
+
+    def slab(j, h):
+        return stage.at[:, :, pl.ds(pl.multiple_of(j * sub + h * part, 128), part)]
+
+    def across(h, k):
+        j = lax.rem(ten + k, n_ten)
+        return pltpu.make_async_remote_copy(
+            src_ref=slab(j, h), dst_ref=mid.at[h, k], send_sem=send_x.at[h, k], recv_sem=recv_x.at[h, k],
+            device_id=(grp, ctx, j), device_id_type=MESH,
+        )
+
+    def along(h, k):
+        return lax.rem(ten + n_ten - k, n_ten), (
+            mid.at[h, k] if k else slab(ten, h),
+            rx.at[h, :, pl.ds(pl.multiple_of(ctx * positions, positions), positions), :],
+            send1.at[h, k], recv1.at[h, ctx],
+        )
 
     def remote(piece, to):
         a, b, s, r = piece
         return pltpu.make_async_remote_copy(
-            src_ref=a, dst_ref=b, send_sem=s, recv_sem=r, device_id=to, device_id_type=MESH
-        )
-
-    for i in [PARTS] + list(range(PARTS)):
-        for j in range(n_ctx):
-            unit, to, pieces = input_copies(j)
-
-            @pl.when(unit != me)
-            def _():
-                remote(pieces[i], to).start()
-
-            @pl.when(unit == me)
-            def _():
-                a, b, s, r = pieces[i]
-                pltpu.make_async_copy(a, b, r).start()
+            src_ref=a, dst_ref=b, send_sem=s, recv_sem=r, device_id=(grp, to, ten), device_id_type=MESH
+        )
+
+    def skip_copy(k):
+        j = lax.rem(ten + k, n_ten)
+        return pltpu.make_async_remote_copy(
+            src_ref=skip_stage.at[:, pl.ds(pl.multiple_of(j * sub, 128), sub)], dst_ref=skip_rx,
+            send_sem=send_skip.at[k], recv_sem=recv_skip.at[0], device_id=(grp, ctx, j), device_id_type=MESH,
+        )
+
+    def start_along(h, k):
+        to, piece = along(h, k)
+
+        @pl.when(to != ctx)
+        def _():
+            remote(piece, to).start()
+
+        @pl.when(to == ctx)
+        def _():
+            pltpu.make_async_copy(piece[0], piece[1], piece[3]).start()
+
+    for k in range(1, n_ten):
+        across(0, k).start()
+    start_along(0, 0)
+
+    @pl.when(ten == ctx)
+    def _():
+        for k in range(1, n_ten):
+            skip_copy(k).start()
+        pltpu.make_async_copy(
+            skip_stage.at[:, pl.ds(pl.multiple_of(ten * sub, 128), sub)], skip_rx, recv_skip.at[0]
+        ).start()
+
+    for h in range(PARTS):
+        if h + 1 < PARTS:
+            for k in range(1, n_ten):
+                across(h + 1, k).start()
+        for k in range(1, n_ten):
+            landed(mid.at[h, k], recv_x.at[h, k])
+            start_along(h, k)
+        if h + 1 < PARTS:
+            start_along(h + 1, 0)
 
     for load in loads[:4]:
         load.wait()
-
-    def landed(ref, sem):
-        pltpu.make_async_copy(ref, ref, sem).wait()
-
-    for p in range(n_ctx):
-        landed(skip_rx.at[p], recv_skip.at[p])
+    landed(skip_rx, recv_skip.at[0])
 
     def gather_copy(h, k):
         here = feats.at[:, pl.ds(pl.multiple_of(ten * sub + h * part, 128), part)]
@@ -194,7 +222,7 @@
             g_high, g_low = gh[:, rows], gl[:, rows]
             acc[...] += mm(g_high, p_high) + mm(g_low, p_high) + mm(g_high, p_low)
 
-        skip = skip_rx[0, 0:1, h * part:(h + 1) * part]
+        skip = skip_rx[0:1, h * part:(h + 1) * part]
         gated = rx[h, 1].astype(jnp.float32) * (
             acc[...] * (1.0 / length) + skip * rx[h, 0].astype(jnp.float32)
         )
@@ -237,13 +265,23 @@
         result = result + rbuf[k].astype(jnp.float32)
     out_ref[...] = result.astype(jnp.bfloat16)
 
-    for i in range(PARTS + 1):
-        for j in range(n_ctx):
-            unit, to, pieces = input_copies(j)
-
-            @pl.when(unit != me)
-            def _():
-                remote(pieces[i], to).wait_send()
+    @pl.when(ten == ctx)
+    def _():
+        for k in range(1, n_ten):
+            skip_copy(k).wait_send()
+
+    def finish_along(h, k):
+        to, piece = along(h, k)
+
+        @pl.when(to != ctx)
+        def _():
+            remote(piece, to).wait_send()
+
+    for h in range(PARTS):
+        for k in range(1, n_ten):
+            across(h, k).wait_send()
+        for k in range(n_ten):
+            finish_along(h, k)
     for h in range(PARTS):
         for k in range(1, n_ten):
             gather_copy(h, k).wait_send()
@@ -258,7 +296,7 @@
     sub = width // n_ctx
     length = n_ctx * positions
     columns = out_weight.shape[1] // n_ten
-    if sub % (PARTS * 128) or length % BLOCK or columns % TILE or positions % 16 or length > 1024:
+    if n_ctx != n_ten or sub % (PARTS * 128) or length % BLOCK or columns % TILE or positions % 16 or length > 1024:
         return body_plain(outer_gate, inner_gate, value_path, long_filter, skip_scale, out_weight)
     tables = [jnp.asarray(t) for t in blocked_tables(length)]
     bf16, f32 = jnp.bfloat16, jnp.float32
@@ -278,17 +316,19 @@
             pltpu.VMEM((length, 2 * length), bf16),
             pltpu.VMEM((length, 2 * length), bf16),
             pltpu.VMEM((3, positions, width), bf16),
+            pltpu.VMEM((PARTS, n_ten, 3, positions, part), bf16),
             pltpu.VMEM((PARTS, 3, length, part), bf16),
             pltpu.VMEM((8, width), f32),
-            pltpu.VMEM((n_ctx, 8, sub), f32),
+            pltpu.VMEM((8, sub), f32),
             pltpu.VMEM((length, part), f32),
             pltpu.VMEM((length, n_ten * sub), bf16),
             pltpu.VMEM((n_ctx, positions, columns), bf16),
             pltpu.VMEM((n_ctx, positions, columns), bf16),
             pltpu.VMEM((positions, columns), f32),
             dma((5,)),
-            dma((PARTS, n_ctx)), dma((PARTS, n_ctx)),
-            dma((n_ctx,)), dma((n_ctx,)),
+            dma((PARTS, n_ten)), dma((PARTS, n_ten)),
+            dma((PARTS, n_ten)), dma((PARTS, n_ctx)),
+            dma((n_ten,)), dma((1,)),
             dma((PARTS, n_ten)), dma((PARTS, n_ten)),
             dma((n_ctx,)), dma((n_ctx,)),
         ],

time: 142 us -> 108 us (0.76)
  Pallas kernels: 140 us -> 104 us
    pallas_call x1, Pallas kernels: 140 us -> 104 us  [body(): pl.pallas_call(functools.partial(fused, n_ctx, n_ten), out_shape=jax.Shap...]
where the time goes in v3:
time: 108 us; the launch traced here: 106 us
  Pallas kernels  104 us (96%)
  local copies, waits for them, and re-layouts  1.88 us (2%)
    pallas_call x1, Pallas kernels, body(): pl.pallas_call(functools.partial(fused, n_ctx, n_ten), out_shape=jax.Shap...  104 us

profile of v3, /device:TPU:9, one launch (start us, length us, event | category | flops | bytes accessed | tf_op | source)
XLA Modules:
  0.0 106.4 jit_solution(14484505392510285000)
XLA Ops:
  0.0 104.5 %shard_map.100 = bf16[128,2048]{1,0:T(8,128)(2,1)} custom-call(bf16[128,2048]{1,0:T(8,128)(2,1)} %outer_ref.1, bf16[128,2048]{1,0:T(8,128)(2,1)} %inner_ref.1, bf16[128,2048]{1,0:T(8,128)(2,1)} %value_ref.1, bf16[128,2048]{1,0:T(8,128)(2,1)} %filter_ref.1, f32[1,2048]{1,0:T(1,128)} %bitcast.1, bf16[2048,8192]{1,0:T(8,128)(2,1)} %w_hbm.1, ...), custom_call_target="tpu_custom_call" | custom-call | tf_op jit(solution)/shard_map/pallas_call | solution.py:307
  104.5 1.9 %copy.12 = bf16[128,2048]{1,0:T(8,128)(2,1)} copy(bf16[128,2048]{1,0:T(8,128)(2,1)} %shard_map.100) | data formatting | bytes 1048576

commit v4 on v3

--- a/solution.py
+++ b/solution.py
@@ -86,7 +86,7 @@
     n_ctx, n_ten,
     outer_ref, inner_ref, value_ref, filter_ref, skip_ref, w_hbm, fh_hbm, fl_hbm, gh_hbm, gl_hbm,
     out_ref,
-    w, fh, fl, gh, gl, stage, mid, rx, skip_stage, skip_rx, acc, feats, pbuf, rbuf, own,
+    w, fh, fl, gh, gl, stage, mid, rx, skip_stage, skip_rx, acc, feats, pbuf, rbuf, own, held,
     load_sem, send_x, recv_x, send1, recv1, send_skip, recv_skip, send2, recv2, send3, recv3,
 ):
     ctx = lax.axis_index("context")
@@ -236,34 +236,63 @@
             came = lax.rem(ten + n_ten - k, n_ten)
             landed(feats.at[:, pl.ds(pl.multiple_of(came * sub + h * part, 128), part)], recv2.at[h, k])
 
-    def partial_copy(k):
-        return pltpu.make_async_remote_copy(
-            src_ref=pbuf.at[k], dst_ref=rbuf.at[k], send_sem=send3.at[k], recv_sem=recv3.at[k],
-            device_id=(grp, lax.rem(ctx + k, n_ctx), ten), device_id_type=MESH,
-        )
-
-    order = sorted(range(1, n_ctx), key=lambda k: abs(k - n_ctx / 2))
-    for k in order + [0]:
-        q = lax.rem(ctx + k, n_ctx)
-        rows = pl.ds(pl.multiple_of(q * positions, positions), positions)
-
+    def partial_copy(q, to, slot):
+        return pltpu.make_async_remote_copy(
+            src_ref=pbuf.at[q], dst_ref=rbuf.at[slot], send_sem=send3.at[q], recv_sem=recv3.at[slot],
+            device_id=(grp, to, ten), device_id_type=MESH,
+        )
+
+    def project(q, dest):
         @pl.loop(0, columns // TILE)
         def _(n):
             cols = pl.ds(pl.multiple_of(n * TILE, TILE), TILE)
-            product = mm(feats[rows, :], w[:, cols])
-            if k == 0:
-                own[:, cols] = product
-            else:
-                pbuf[k, :, cols] = product.astype(jnp.bfloat16)
-
-        if k:
-            partial_copy(k).start()
-
-    result = own[...]
-    for k in order:
-        landed(rbuf.at[k], recv3.at[k])
-        result = result + rbuf[k].astype(jnp.float32)
-    out_ref[...] = result.astype(jnp.bfloat16)
+            product = mm(feats[q * positions:(q + 1) * positions, :], w[:, cols])
+            dest[:, cols] = product.astype(dest.dtype)
+
+    def exchange(role):
+        copies = []
+
+        def send(q, to, slot):
+            copies.append(partial_copy(q, to, slot))
+            copies[-1].start()
+
+        if role in (0, 3):
+            near, third, far = (1, 2, 3) if role == 0 else (2, 1, 0)
+            project(far, pbuf.at[far])
+            send(far, near, near)
+            project(third, pbuf.at[third])
+            send(third, third, role)
+            project(near, pbuf.at[near])
+            send(near, near, role)
+            project(role, own)
+            expected = (near, third)
+        else:
+            peer = 3 - role
+            near = 0 if role == 1 else 3
+            far = 3 - near
+            project(peer, pbuf.at[peer])
+            send(peer, peer, role)
+            project(far, held)
+            project(near, pbuf.at[near])
+            send(near, near, role)
+            project(role, own)
+            landed(rbuf.at[role], recv3.at[role])
+            pbuf[far] = (held[...] + rbuf[role].astype(jnp.float32)).astype(jnp.bfloat16)
+            send(far, far, role)
+            expected = (near, peer, far)
+        result = own[...]
+        for slot in expected:
+            landed(rbuf.at[slot], recv3.at[slot])
+            result = result + rbuf[slot].astype(jnp.float32)
+        out_ref[...] = result.astype(jnp.bfloat16)
+        for copy in copies:
+            copy.wait_send()
+
+    for role in range(n_ctx):
+
+        @pl.when(ctx == role)
+        def _():
+            exchange(role)
 
     @pl.when(ten == ctx)
     def _():
@@ -285,8 +314,6 @@
     for h in range(PARTS):
         for k in range(1, n_ten):
             gather_copy(h, k).wait_send()
-    for k in order:
-        partial_copy(k).wait_send()
 
 
 def body(outer_gate, inner_gate, value_path, long_filter, skip_scale, out_weight):
@@ -296,7 +323,7 @@
     sub = width // n_ctx
     length = n_ctx * positions
     columns = out_weight.shape[1] // n_ten
-    if n_ctx != n_ten or sub % (PARTS * 128) or length % BLOCK or columns % TILE or positions % 16 or length > 1024:
+    if n_ctx != 4 or n_ctx != n_ten or sub % (PARTS * 128) or length % BLOCK or columns % TILE or positions % 16 or length > 1024:
         return body_plain(outer_gate, inner_gate, value_path, long_filter, skip_scale, out_weight)
     tables = [jnp.asarray(t) for t in blocked_tables(length)]
     bf16, f32 = jnp.bfloat16, jnp.float32
@@ -325,6 +352,7 @@
             pltpu.VMEM((n_ctx, positions, columns), bf16),
             pltpu.VMEM((n_ctx, positions, columns), bf16),
             pltpu.VMEM((positions, columns), f32),
+            pltpu.VMEM((positions, columns), f32),
             dma((5,)),
             dma((PARTS, n_ten)), dma((PARTS, n_ten)),
             dma((PARTS, n_ten)), dma((PARTS, n_ctx)),

time: 108 us -> 104 us (0.963); the launches traced: 106 us -> 104 us
  Pallas kernels: 104 us -> 102 us
    pallas_call x1, Pallas kernels: 104 us -> 102 us  [body(): pl.pallas_call(functools.partial(fused, n_ctx, n_ten), out_shape=jax.Shap...]
where the time goes in v4:
time: 104 us
  Pallas kernels  102 us (98%)
  local copies, waits for them, and re-layouts  1.88 us (2%)
    pallas_call x1, Pallas kernels, body(): pl.pallas_call(functools.partial(fused, n_ctx, n_ten), out_shape=jax.Shap...  102 us

profile of v4, /device:TPU:9, one launch (start us, length us, event | category | flops | bytes accessed | tf_op | source)
XLA Modules:
  0.0 103.9 jit_solution(1361298382460709422)
XLA Ops:
  0.0 102.0 %shard_map.100 = bf16[128,2048]{1,0:T(8,128)(2,1)} custom-call(bf16[128,2048]{1,0:T(8,128)(2,1)} %outer_ref.1, bf16[128,2048]{1,0:T(8,128)(2,1)} %inner_ref.1, bf16[128,2048]{1,0:T(8,128)(2,1)} %value_ref.1, bf16[128,2048]{1,0:T(8,128)(2,1)} %filter_ref.1, f32[1,2048]{1,0:T(1,128)} %bitcast.1, bf16[2048,8192]{1,0:T(8,128)(2,1)} %w_hbm.1, ...), custom_call_target="tpu_custom_call" | custom-call | tf_op jit(solution)/shard_map/pallas_call | solution.py:334
  102.0 1.9 %copy.12 = bf16[128,2048]{1,0:T(8,128)(2,1)} copy(bf16[128,2048]{1,0:T(8,128)(2,1)} %shard_map.100) | data formatting | bytes 1048576

commit v5 on v4

--- a/solution.py
+++ b/solution.py
@@ -66,7 +66,7 @@
 
 
 MESH = pl.DeviceIdType.MESH
-PARTS = 2
+PARTS = 4
 BLOCK = 128
 TILE = 256
 

time: 104 us -> 98.2 us (0.944)
  Pallas kernels: 102 us -> 96.2 us
    pallas_call x1, Pallas kernels: 102 us -> 96.2 us  [body(): pl.pallas_call(functools.partial(fused, n_ctx, n_ten), out_shape=jax.Shap...]
where the time goes in v5:
time: 98.2 us; the launch traced here: 98 us
  Pallas kernels  96.2 us (98%)
  local copies, waits for them, and re-layouts  1.88 us (2%)
    pallas_call x1, Pallas kernels, body(): pl.pallas_call(functools.partial(fused, n_ctx, n_ten), out_shape=jax.Shap...  96.2 us

profile of v5, /device:TPU:9, one launch (start us, length us, event | category | flops | bytes accessed | tf_op | source)
XLA Modules:
  0.0 98.0 jit_solution(2284099969529034937)
XLA Ops:
  0.0 96.2 %shard_map.100 = bf16[128,2048]{1,0:T(8,128)(2,1)} custom-call(bf16[128,2048]{1,0:T(8,128)(2,1)} %outer_ref.1, bf16[128,2048]{1,0:T(8,128)(2,1)} %inner_ref.1, bf16[128,2048]{1,0:T(8,128)(2,1)} %value_ref.1, bf16[128,2048]{1,0:T(8,128)(2,1)} %filter_ref.1, f32[1,2048]{1,0:T(1,128)} %bitcast.1, bf16[2048,8192]{1,0:T(8,128)(2,1)} %w_hbm.1, ...), custom_call_target="tpu_custom_call" | custom-call | tf_op jit(solution)/shard_map/pallas_call | solution.py:334
  96.2 1.9 %copy.12 = bf16[128,2048]{1,0:T(8,128)(2,1)} copy(bf16[128,2048]{1,0:T(8,128)(2,1)} %shard_map.100) | data formatting | bytes 1048576

commit v6 on v5

--- a/solution.py
+++ b/solution.py
@@ -211,9 +211,9 @@
         def _(b):
             rows = pl.ds(pl.multiple_of(b * 2 * BLOCK, 2 * BLOCK), 2 * BLOCK)
             f_high, f_low = fh[rows, :], fl[rows, :]
-            signal, kernel = rx[h, 0], rx[h, 2]
-            spec_s = mm(f_high, signal) + mm(f_low, signal)
-            spec_k = mm(f_high, kernel) + mm(f_low, kernel)
+            both = jnp.concatenate([rx[h, 0], rx[h, 2]], axis=1)
+            spec = mm(f_high, both) + mm(f_low, both)
+            spec_s, spec_k = spec[:, :part], spec[:, part:]
             s_re, s_im = spec_s[:BLOCK], spec_s[BLOCK:]
             k_re, k_im = spec_k[:BLOCK], spec_k[BLOCK:]
             prod = jnp.concatenate([s_re * k_re - s_im * k_im, s_re * k_im + s_im * k_re], axis=0)

time: 98.2 us -> 97.7 us (level)
  no operation moved by 1% of the time
where the time goes in v6:
time: 97.7 us; the launch traced here: 97.5 us
  Pallas kernels  95.6 us (98%)
  local copies, waits for them, and re-layouts  1.88 us (2%)
    pallas_call x1, Pallas kernels, body(): pl.pallas_call(functools.partial(fused, n_ctx, n_ten), out_shape=jax.Shap...  95.6 us

profile of v6, /device:TPU:9, one launch (start us, length us, event | category | flops | bytes accessed | tf_op | source)
XLA Modules:
  0.0 97.5 jit_solution(12382158219226337009)
XLA Ops:
  0.0 95.6 %shard_map.100 = bf16[128,2048]{1,0:T(8,128)(2,1)} custom-call(bf16[128,2048]{1,0:T(8,128)(2,1)} %outer_ref.1, bf16[128,2048]{1,0:T(8,128)(2,1)} %inner_ref.1, bf16[128,2048]{1,0:T(8,128)(2,1)} %value_ref.1, bf16[128,2048]{1,0:T(8,128)(2,1)} %filter_ref.1, f32[1,2048]{1,0:T(1,128)} %bitcast.1, bf16[2048,8192]{1,0:T(8,128)(2,1)} %w_hbm.1, ...), custom_call_target="tpu_custom_call" | custom-call | tf_op jit(solution)/shard_map/pallas_call | solution.py:334
  95.6 1.9 %copy.12 = bf16[128,2048]{1,0:T(8,128)(2,1)} copy(bf16[128,2048]{1,0:T(8,128)(2,1)} %shard_map.100) | data formatting | bytes 1048576
